TPU v7x, 256 devices: a whole 4x4x8 slice. The times are simulated.
256 devices in a mesh: dp: 32 (over y, x, core), seq: 8 (over z).
Axes of the slice: x: 4, y: 4, z: 8, core: 2. Of those that a mesh axis runs over, the one named last changes fastest.
Arguments:
- hidden_in: bfloat16 [32, 8, 128, 4096], P('dp', 'seq'), may hold values from -6 to 6
- queries: bfloat16 [32, 8, 128, 4096], P('dp', 'seq'), may hold values from -110 to 110
- keys: bfloat16 [32, 8, 128, 512], P('dp', 'seq'), may hold values from -4.5 to 4.5
- values: bfloat16 [32, 8, 128, 512], P('dp', 'seq'), may hold values from -6 to 6
- out_grad: bfloat16 [32, 8, 128, 4096], P('dp', 'seq'), may hold values from -6 to 6
- parents: int32 [32, 8], P('dp', 'seq'), may hold values from 0 to 6, as said below
- counts: int32 [32, 8], P('dp', 'seq'), may hold values from 64 to 128, as said below
Outputs:
- query_grad: bfloat16 [32, 8, 128, 4096], P('dp', 'seq')
- key_grad: bfloat16 [32, 8, 128, 512], P('dp', 'seq')
- value_grad: bfloat16 [32, 8, 128, 512], P('dp', 'seq')
- weight_grad: float32 [4096, 512], P(('dp', 'seq'))
Inputs may be any that keep to these rules, and one draw needn't show every extreme that they name: `parents`: segment 0 is its own parent; any other segment i has a parent below i; the last segment's parent is segment 8 - 2. `counts`: at least 64 tokens of each segment are live; some segment of every tree is full.
All inputs are finite; a program needn't handle non-finite values.
Results may differ from a plain program's by a relative error of at most 0.018.
Values may be sent and summed in bfloat16 or wider, within the bound.
No kernel may reach another device: no remote copies, remote signals or barrier semaphores. Data moves between devices by JAX's collectives and lax.ppermute only.
A program may use at most 64 MiB of HBM per device.

v0:
```python
import jax
import jax.numpy as jnp
from jax import lax
from jax.sharding import PartitionSpec as P

KV_HEAD_COUNT = 4
HEAD_SIZE = 128
QUERY_PER_KV = 8


NEG_FILL = -1e30


def local(hidden_in, queries, keys, values, out_grad, parents, counts):
    seg_len = keys.shape[2]
    head_dim = HEAD_SIZE
    key_value_heads = KV_HEAD_COUNT
    group_size = QUERY_PER_KV
    score_scale = 1.0 / HEAD_SIZE**0.5
    seg_total = lax.axis_size("seq")
    my_index = lax.axis_index("seq")
    tree_parents, tree_counts = (
        lax.all_gather(parents, "seq", axis=1, tiled=True),
        lax.all_gather(counts, "seq", axis=1, tiled=True),
    )
    tree_parents = tree_parents[0]
    tree_counts = tree_counts[0]
    key_whole, value_whole = (
        lax.all_gather(keys, "seq", axis=1, tiled=True),
        lax.all_gather(values, "seq", axis=1, tiled=True),
    )
    token_count_total = seg_total * seg_len
    key_pieces = key_whole.reshape(token_count_total, key_value_heads, head_dim).transpose(1, 0, 2)
    value_pieces = value_whole.reshape(token_count_total, key_value_heads, head_dim).transpose(
        1, 0, 2
    )
    labels = jnp.arange(seg_total, dtype=jnp.int32)

    def climb(level, state):
        current, reached = state
        current = jnp.sum(jnp.where(labels == current, tree_parents, 0))
        return (current, reached | (labels == current))

    start_state = (my_index, jnp.zeros((seg_total,), dtype=bool))
    ignored, reached = lax.fori_loop(0, seg_total - 1, climb, start_state)
    earlier = reached & (labels != my_index)
    positions = jnp.arange(seg_len, dtype=jnp.int32)
    key_live = (positions[None, :] < tree_counts[:, None]).reshape(token_count_total)
    key_earlier = jnp.repeat(earlier, seg_len)
    key_own = jnp.repeat(labels == my_index, seg_len)
    key_position = jnp.tile(positions, seg_total)
    my_count = jnp.sum(jnp.where(labels == my_index, tree_counts, 0))
    row_live = positions < my_count
    allowed = (
        row_live[:, None]
        & key_live[None, :]
        & (key_earlier[None, :] | key_own[None, :] & (key_position[None, :] <= positions[:, None]))
    )
    query_pieces = queries.reshape(seg_len, key_value_heads, group_size, head_dim).transpose(
        1, 2, 0, 3
    )
    split_gradient = out_grad.reshape(seg_len, key_value_heads, group_size, head_dim).transpose(
        1, 2, 0, 3
    )

    def group_stats(query_head, grad_head, key_head, value_head):
        scores = (
            jnp.einsum("hqd,kd->hqk", query_head, key_head, preferred_element_type=jnp.float32)
            * score_scale
        )
        scores = jnp.where(allowed[None], scores, NEG_FILL)
        row_top = jnp.max(scores, axis=-1, keepdims=True)
        weights = jnp.where(allowed[None], jnp.exp(scores - row_top), 0.0)
        row_total = jnp.sum(weights, axis=-1, keepdims=True)
        row_total = jnp.where(row_live[None, :, None], row_total, 1.0)
        normed = weights / row_total
        normed_low = lax.optimization_barrier(normed.astype(jnp.bfloat16))
        attended = jnp.einsum(
            "hqk,kd->hqd", normed_low, value_head, preferred_element_type=jnp.float32
        )
        row_delta = jnp.sum(grad_head.astype(jnp.float32) * attended, axis=-1, keepdims=True)
        grad_probs = jnp.einsum(
            "hqd,kd->hqk", grad_head, value_head, preferred_element_type=jnp.float32
        )
        grad_scores = lax.optimization_barrier(
            (normed * (grad_probs - row_delta)).astype(jnp.bfloat16)
        )
        query_gradient = (
            jnp.einsum("hqk,kd->hqd", grad_scores, key_head, preferred_element_type=jnp.float32)
            * score_scale
        ).astype(jnp.bfloat16)
        return (normed_low, grad_scores, query_gradient, row_top, row_total, row_delta)

    def key_side(normed_low, grad_scores, query_head, grad_head):
        key_gradient = (
            jnp.einsum("hqk,hqd->kd", grad_scores, query_head, preferred_element_type=jnp.float32)
            * score_scale
        )
        value_gradient = jnp.einsum(
            "hqk,hqd->kd", normed_low, grad_head, preferred_element_type=jnp.float32
        )
        return (key_gradient, value_gradient)

    def dense_group(pieces):
        query_head, grad_head, key_head, value_head = pieces
        normed_low, grad_scores, query_gradient, row_top, row_total, row_delta = group_stats(
            query_head, grad_head, key_head, value_head
        )
        key_gradient, value_gradient = key_side(normed_low, grad_scores, query_head, grad_head)
        return (query_gradient, key_gradient, value_gradient)

    query_gradient, key_gradient, value_gradient = lax.map(
        dense_group, (query_pieces, split_gradient, key_pieces, value_pieces)
    )
    key_rows = key_gradient.transpose(1, 0, 2).reshape(
        token_count_total, key_value_heads * head_dim
    )
    value_rows = value_gradient.transpose(1, 0, 2).reshape(
        token_count_total, key_value_heads * head_dim
    )
    partial_value = jnp.concatenate([key_rows, value_rows], axis=1)
    owned_grads = lax.psum_scatter(partial_value, "seq", scatter_dimension=0, tiled=True)
    query_out = query_gradient.transpose(2, 0, 1, 3).reshape(
        1, 1, seg_len, key_value_heads * group_size * head_dim
    )
    key_reduced = owned_grads[:, : key_value_heads * head_dim].astype(jnp.bfloat16)
    value_reduced = owned_grads[:, key_value_heads * head_dim :].astype(jnp.bfloat16)
    hidden_rows = hidden_in.reshape(seg_len, hidden_in.shape[3])
    weight_grad = lax.psum_scatter(
        lax.dot_general(
            hidden_rows, key_reduced, (((0,), (0,)), ((), ())), preferred_element_type=jnp.float32
        ),
        ("dp", "seq"),
        scatter_dimension=0,
        tiled=True,
    )
    key_out = key_reduced.reshape(1, 1, seg_len, key_value_heads * head_dim)
    value_out = value_reduced.reshape(1, 1, seg_len, key_value_heads * head_dim)
    return (query_out, key_out, value_out, weight_grad)


def solution(mesh):
    placed = (
        P("dp", "seq", None, None),
        P("dp", "seq", None, None),
        P("dp", "seq", None, None),
        P("dp", "seq", None, None),
        P("dp", "seq", None, None),
        P("dp", "seq"),
        P("dp", "seq"),
    )
    return jax.shard_map(
        local,
        mesh=mesh,
        in_specs=placed,
        out_specs=(
            P("dp", "seq", None, None),
            P("dp", "seq", None, None),
            P("dp", "seq", None, None),
            P(("dp", "seq"), None),
        ),
        check_vma=False,
    )
```

profile of v0, /device:TPU:0, one launch (start us, length us, event | category | flops | bytes accessed | tf_op | source)
XLA Modules:
  0.0 1523.3 jit_solution(18382030940761315404)
XLA Ops:
  7.2 0.7 all-gather.3.cloned.1.call-update
  8.0 0.7 all-gather.5.cloned.1.call-update
  10.0 1.3 dynamic-slice
  11.3 0.7 bitcast_dynamic-update-slice_fusion.1
  12.0 0.7 bitcast_dynamic-update-slice_fusion
  12.7 14.5 all-reduce.2
  27.2 13.7 while.30
  27.8 0.7 select_or_fusion.2
  29.8 0.7 select_or_fusion.2
  31.7 0.7 select_or_fusion.2
  33.7 0.7 select_or_fusion.2
  35.6 0.7 select_or_fusion.2
  37.6 0.7 select_or_fusion.2
  39.6 0.7 select_or_fusion.2
  40.9 2.3 copy.39
  43.3 0.7 copy.42
  45.5 4.2 all-gather.3.cloned.1.call-done
  49.7 1.3 reshape.106
  51.0 1.1 copy.73
  52.1 36.6 %all-gather.5.cloned.1.call-done = bf16[1,8,128,512]{3,2,0,1:T(8,128)(2,1)} async-done(((bf16[1,1,128,512]{3,2,0,1:T(8,128)(2,1)}), bf16[1,8,128,512]{3,2,0,1:T(8,128)(2,1)}) %all-gather.5.cloned.1.call-update) | async-done | bytes 1048592 | tf_op jit(solution)/shard_map/all_gather | solution.py:30
  88.7 1.3 reshape.107
  90.1 1.1 copy.72
  91.2 68.3 %while.29 = (s32[]{:T(128)}, bf16[4,8,128,128]{3,2,1,0:T(8,128)(2,1)}, f32[4,1024,128]{2,1,0:T(8,128)}, f32[4,1024,128]{2,1,0:T(8,128)}, bf16[4,8,128,128]{2,3,1...) while((s32[]{:T(128)}, ...), condition=%wide.region_8.9_spmd.clone, body=%wide.region_4.8_spmd.clone.sunk | while | flops 1623590016 | bytes 51290712 | solution.py:112
  91.2 0.6 iota_compare_fusion.5
  92.2 4.9 fusion.115
  97.1 2.9 fusion.116
  100.0 0.8 fusion.117
  100.9 0.9 multiply_convert_fusion.2
  101.8 1.6 fusion.120
  103.4 2.4 fusion.118
  105.8 2.5 fusion.119
  109.3 4.9 fusion.115
  114.2 2.9 fusion.116
  117.1 0.8 fusion.117
  118.0 0.9 multiply_convert_fusion.2
  118.9 1.6 fusion.120
  120.5 2.4 fusion.118
  122.8 2.5 fusion.119
  126.4 4.9 fusion.115
  131.3 2.9 fusion.116
  134.2 0.8 fusion.117
  135.1 0.9 multiply_convert_fusion.2
  136.0 1.5 fusion.120
  137.5 2.4 fusion.118
  139.9 2.5 fusion.119
  142.4 0.6 iota_compare_fusion.5
  143.4 4.9 fusion.115
  148.3 2.9 fusion.116
  151.2 0.8 fusion.117
  152.1 0.9 multiply_convert_fusion.2
  153.0 1.6 fusion.120
  154.6 2.4 fusion.118
  157.0 2.5 fusion.119
  159.5 2.8 copy_bitcast_fusion
  162.3 2.3 pad_maximum_fusion
  164.7 53.9 %reduce-scatter.5.cloned.1.call-done = f32[128,1024]{1,0:T(8,128)} async-done(((f32[1024,1024]{1,0:T(8,128)}), f32[128,1024]{1,0:T(8,128)}) %reduce-scatter.5.cloned.1.call-update) | async-done | bytes 524304 | tf_op jit(solution)/shard_map/reduce_scatter | solution.py:122
  218.6 1.1 convert.4
  219.7 4.5 convolution_bitcast_fusion.2
  224.2 9.0 copy.62
  233.2 1.2 copy-done.4
  234.4 0.7 copy.49
  235.1 1.3 reshape.83
  236.3 0.7 slice_bitcast_fusion
  237.0 1279.8 %reduce-scatter.7.cloned.1.call-done = f32[16,512]{1,0:T(8,128)} async-done(((f32[4096,512]{1,0:T(8,128)}), f32[16,512]{1,0:T(8,128)}) %reduce-scatter.7.cloned.1.call-update) | async-done | bytes 32784
  (66 shorter events, 9.4 us)
Async XLA Ops:
  7.2 212.5 %copy-start = (bf16[1,1,128,4096]{3,2,1,0:T(8,128)(2,1)S(1)}, bf16[1,1,128,4096]{3,2,1,0:T(8,128)(2,1)}, u32[]{:S(2)}) copy-start(bf16[1,1,128,4096]{3,2,1,0:T(8,128)(2,1)} %param.11) | copy-start | bytes 3145732
  7.2 36.1 %copy-start.2 = (bf16[1,1,128,4096]{3,2,1,0:T(8,128)(2,1)S(1)}, bf16[1,1,128,4096]{3,2,1,0:T(8,128)(2,1)}, u32[]{:S(2)}) copy-start(bf16[1,1,128,4096]{3,2,1,0:T(8,128)(2,1)} %param.15) | copy-start | bytes 3145732
  7.2 42.5 %all-gather.3.cloned.1.call-start = ((), (), s32[]{:S(2)}) async-start(), calls=%async_computation.2 | async-start | bytes 1179648 | tf_op jit(solution)/shard_map/all_gather | solution.py:29
  7.9 80.8 %all-gather.5.cloned.1.call-start = ((), (), s32[]{:S(2)}) async-start(), calls=%async_computation.3 | async-start | bytes 1179648 | tf_op jit(solution)/shard_map/all_gather | solution.py:30
  8.7 209.9 %reduce-scatter.5.cloned.1.call-start = ((), (), s32[]{:S(2)}) async-start(), calls=%async_computation.4 | async-start | bytes 4718592 | tf_op jit(solution)/shard_map/reduce_scatter | solution.py:122
  97.1 2.9 copy-start.3
  97.1 3.8 copy-start.1
  114.2 2.9 copy-start.3
  114.2 3.8 copy-start.1
  131.3 2.9 copy-start.3
  131.3 3.8 copy-start.1
  148.3 2.9 copy-start.3
  148.3 3.8 copy-start.1
  164.7 1352.2 %reduce-scatter.7.cloned.1.call-start = ((), (), s32[]{:S(2)}) async-start(), calls=%async_computation.5 | async-start | bytes 8421376
  233.1 1.2 copy-start.4
Sparse Core Ops, SparseCore 0:
  9.8 39.7 all-gather.2
  51.4 37.2 all-gather.4
  164.8 53.7 reduce-scatter.4
  233.3 1283.4 reduce-scatter.6
where the time goes:
time: 1520 us
  waiting for transfers between devices  1380 us (91%)
  matrix products  56.6 us (4%)
  other arithmetic  28.5 us (2%)
  local copies, waits for them, and re-layouts  27.6 us (2%)
    unnamed x5, waiting for transfers between devices  1280 us
    reduce_scatter x1, waiting for transfers between devices, local(): lax.psum_scatter(partial_value, 'seq', scatter_dimension=0, tiled=True)  53.9 us
    all_gather x1, waiting for transfers between devices, local(): lax.all_gather(values, 'seq', axis=1, tiled=True)  36.6 us
  transfers between devices with their start and end apart: 4, of which 4 were waited for; matrix products, arithmetic and copies ran while one was open for 1% of the time, Pallas kernels for 0%

commit v1 on v0

v1 whole, which is shorter than its diff:
```python
import functools
import math

import jax
import jax.numpy as jnp
from jax import lax
from jax.experimental import pallas as pl
from jax.experimental.pallas import tpu as pltpu
from jax.sharding import PartitionSpec as P

SEGMENTS = 8
SEG_LEN = 128
KV_HEADS = 4
GROUP = 8
HEAD = 128
KV_COLS = KV_HEADS * HEAD
Q_COLS = KV_HEADS * GROUP * HEAD
GROUP_COLS = GROUP * HEAD
PAIR = 2
SCALE = 1.0 / math.sqrt(HEAD)
SCALE_LOG2 = SCALE * math.log2(math.e)
NEG_FILL = -1e30
DEAD_LSE = 1e30
BF16 = jnp.bfloat16
F32 = jnp.float32

X, Y, CORES = 4, 4, 2


def dot_nt(a, b):
    return lax.dot_general(a, b, (((1,), (1,)), ((), ())), preferred_element_type=F32)


def dot_nn(a, b):
    return lax.dot_general(a, b, (((1,), (0,)), ((), ())), preferred_element_type=F32)


def dot_tn(a, b):
    return lax.dot_general(a, b, (((0,), (0,)), ((), ())), preferred_element_type=F32)


def is_ancestor(meta_ref, me, segment):
    current = me
    hit = segment < 0
    for _ in range(SEGMENTS - 1):
        current = meta_ref[current]
        hit = hit | (current == segment)
    return hit & (segment != me)


def stacked(ref, pair):
    first = pair * PAIR * HEAD
    return jnp.concatenate(
        [ref[:, first + i * HEAD : first + (i + 1) * HEAD] for i in range(PAIR)], axis=0
    )


def key_bias(live):
    position = lax.broadcasted_iota(jnp.int32, (SEG_LEN, 1), 0)
    return jnp.where(position < live, 0.0, NEG_FILL).astype(F32)


def own_bias(live):
    key_at = lax.broadcasted_iota(jnp.int32, (SEG_LEN, PAIR * SEG_LEN), 0)
    query_at = lax.broadcasted_iota(jnp.int32, (SEG_LEN, PAIR * SEG_LEN), 1) & (SEG_LEN - 1)
    return jnp.where((key_at <= query_at) & (key_at < live), 0.0, NEG_FILL).astype(F32)


def segment_id(me, offset):
    return lax.rem(me + (offset + SEGMENTS), SEGMENTS)


def stats_kernel(offsets, first, last, *refs):
    meta_ref, q_ref, g_ref = refs[:3]
    kv_refs = refs[3 : 3 + 2 * len(offsets)]
    rest = refs[3 + 2 * len(offsets) :]
    if first:
        (out_ref,) = rest
    else:
        in_ref, out_ref = rest
    me = meta_ref[2 * SEGMENTS]

    def add_segment(source_ref, k_ref, v_ref, bias, start):
        k, v = k_ref[...], v_ref[...]
        for pair in range(GROUP // PAIR):
            cols = slice(pair * PAIR * HEAD, (pair + 1) * PAIR * HEAD)
            scores = dot_nt(k, stacked(q_ref, pair)) * SCALE_LOG2 + bias
            grad_probs = dot_nt(v, stacked(g_ref, pair))
            top = jnp.max(scores, axis=0, keepdims=True)
            if not start:
                old_top = source_ref[0:1, cols]
                top = jnp.maximum(top, old_top)
            weights = jnp.exp2(scores - top)
            total = jnp.sum(weights, axis=0, keepdims=True)
            mixed = jnp.sum(weights * grad_probs, axis=0, keepdims=True)
            if not start:
                shrink = jnp.exp2(old_top - top)
                total = total + source_ref[1:2, cols] * shrink
                mixed = mixed + source_ref[2:3, cols] * shrink
            out_ref[0:1, cols] = top
            out_ref[1:2, cols] = total
            out_ref[2:3, cols] = mixed

    if first:
        add_segment(
            None, kv_refs[0], kv_refs[1], own_bias(meta_ref[SEGMENTS + me]), True
        )
    else:
        out_ref[...] = in_ref[...]
        for i, offset in enumerate(offsets):
            segment = segment_id(me, offset)

            @pl.when(is_ancestor(meta_ref, me, segment))
            def _():
                add_segment(
                    out_ref,
                    kv_refs[2 * i],
                    kv_refs[2 * i + 1],
                    key_bias(meta_ref[SEGMENTS + segment]),
                    False,
                )

    if last:
        live = meta_ref[SEGMENTS + me]
        position = lax.broadcasted_iota(jnp.int32, (1, GROUP_COLS), 1) & (SEG_LEN - 1)
        total = out_ref[1:2, :]
        row_delta = out_ref[2:3, :] / total
        lse = out_ref[0:1, :] + jnp.log2(total)
        out_ref[0:1, :] = jnp.where(position < live, lse, DEAD_LSE)
        out_ref[1:2, :] = row_delta


def grads_kernel(offsets, first, last, *refs):
    meta_ref, q_ref, g_ref, stats_ref = refs[:4]
    count = len(offsets)
    kv_refs = refs[4 : 4 + 2 * count]
    rest = refs[4 + 2 * count :]
    if first:
        acc_ref, *out_refs = rest
    elif last:
        in_ref, dq_ref, *out_refs, acc_ref = rest
    else:
        in_ref, acc_ref, *out_refs = rest
    me = meta_ref[2 * SEGMENTS]
    if first:
        acc_ref[...] = jnp.zeros_like(acc_ref)
    else:
        acc_ref[...] = in_ref[...]

    def add_segment(k_ref, v_ref, dk_ref, dv_ref, bias):
        k, v = k_ref[...], v_ref[...]
        dk = jnp.zeros((SEG_LEN, HEAD), F32)
        dv = jnp.zeros((SEG_LEN, HEAD), F32)
        for pair in range(GROUP // PAIR):
            cols = slice(pair * PAIR * HEAD, (pair + 1) * PAIR * HEAD)
            q_pair = stacked(q_ref, pair)
            g_pair = stacked(g_ref, pair)
            scores = dot_nt(k, q_pair) * SCALE_LOG2 + bias
            probs = jnp.exp2(scores - stats_ref[0:1, cols])
            grad_probs = dot_nt(v, g_pair)
            grad_scores = (probs * (grad_probs - stats_ref[1:2, cols])).astype(BF16)
            dv += dot_nn(probs.astype(BF16), g_pair)
            dk += dot_nn(grad_scores, q_pair)
            dq = dot_tn(grad_scores, k)
            for i in range(PAIR):
                head = slice((pair * PAIR + i) * HEAD, (pair * PAIR + i + 1) * HEAD)
                acc_ref[:, head] += dq[i * SEG_LEN : (i + 1) * SEG_LEN]
        dk_ref[...] = (dk * SCALE).astype(dk_ref.dtype)
        dv_ref[...] = dv.astype(dv_ref.dtype)

    for i, offset in enumerate(offsets):
        dk_ref, dv_ref = out_refs[2 * i], out_refs[2 * i + 1]
        if offset == 0:
            add_segment(
                kv_refs[2 * i], kv_refs[2 * i + 1], dk_ref, dv_ref, own_bias(meta_ref[SEGMENTS + me])
            )
        else:
            segment = segment_id(me, offset)
            seen = is_ancestor(meta_ref, me, segment)

            @pl.when(seen)
            def _():
                add_segment(
                    kv_refs[2 * i],
                    kv_refs[2 * i + 1],
                    dk_ref,
                    dv_ref,
                    key_bias(meta_ref[SEGMENTS + segment]),
                )

            @pl.when(jnp.logical_not(seen))
            def _():
                dk_ref[...] = jnp.zeros_like(dk_ref)
                dv_ref[...] = jnp.zeros_like(dv_ref)

    if last:
        dq_ref[...] = (acc_ref[...] * SCALE).astype(BF16)


SMEM_SPEC = pl.BlockSpec(memory_space=pltpu.SMEM)
Q_SPEC = pl.BlockSpec((SEG_LEN, GROUP_COLS), lambda g: (0, g))
STATS_SPEC = pl.BlockSpec((8, GROUP_COLS), lambda g: (0, g))
K_SPEC = pl.BlockSpec((SEG_LEN, HEAD), lambda g: (0, g))
V_SPEC = pl.BlockSpec((SEG_LEN, HEAD), lambda g: (0, g + KV_HEADS))
STATS_SHAPE = jax.ShapeDtypeStruct((8, Q_COLS), F32)
BLOCK_FLOPS = 2 * SEG_LEN * SEG_LEN * HEAD * KV_HEADS * GROUP


def add_stats(meta, q, g, packets, offsets, stats, last=False):
    first = stats is None
    operands = [meta, q, g]
    specs = [SMEM_SPEC, Q_SPEC, Q_SPEC]
    for packet in packets:
        operands += [packet, packet]
        specs += [K_SPEC, V_SPEC]
    if not first:
        operands.append(stats)
        specs.append(STATS_SPEC)
    return pl.pallas_call(
        functools.partial(stats_kernel, tuple(offsets), first, last),
        grid=(KV_HEADS,),
        out_shape=STATS_SHAPE,
        in_specs=specs,
        out_specs=STATS_SPEC,
        name="stats",
        cost_estimate=pl.CostEstimate(
            flops=4 * BLOCK_FLOPS * len(packets),
            bytes_accessed=4 * SEG_LEN * Q_COLS,
            transcendentals=SEG_LEN * SEG_LEN * KV_HEADS * GROUP * len(packets),
        ),
        compiler_params=pltpu.CompilerParams(vmem_limit_bytes=32 << 20),
    )(*operands)


def add_grads(meta, q, g, stats, packets, offsets, acc, out_dtype, last=False):
    first = acc is None
    operands = [meta, q, g, stats]
    specs = [SMEM_SPEC, Q_SPEC, Q_SPEC, STATS_SPEC]
    for packet in packets:
        operands += [packet, packet]
        specs += [K_SPEC, V_SPEC]
    aliases = {}
    if not first:
        if not last:
            aliases = {len(operands): 0}
        operands.append(acc)
        specs.append(Q_SPEC)
    out_shapes = [jax.ShapeDtypeStruct((SEG_LEN, Q_COLS), BF16 if last else F32)]
    out_specs = [Q_SPEC]
    for _ in packets:
        out_shapes += [jax.ShapeDtypeStruct((SEG_LEN, KV_COLS), out_dtype)] * 2
        out_specs += [K_SPEC] * 2
    outs = pl.pallas_call(
        functools.partial(grads_kernel, tuple(offsets), first, last),
        grid=(KV_HEADS,),
        out_shape=out_shapes,
        in_specs=specs,
        out_specs=out_specs,
        scratch_shapes=[pltpu.VMEM((SEG_LEN, GROUP_COLS), F32)] if last else [],
        input_output_aliases=aliases,
        name="grads",
        cost_estimate=pl.CostEstimate(
            flops=10 * BLOCK_FLOPS * len(packets),
            bytes_accessed=12 * SEG_LEN * Q_COLS,
            transcendentals=SEG_LEN * SEG_LEN * KV_HEADS * GROUP * len(packets),
        ),
        compiler_params=pltpu.CompilerParams(vmem_limit_bytes=32 << 20),
    )(*operands)
    return outs[0], [(outs[1 + 2 * i], outs[2 + 2 * i]) for i in range(len(packets))]


def shift_seq(array, k):
    return lax.ppermute(array, "seq", [(i, (i + k) % SEGMENTS) for i in range(SEGMENTS)])


def swap_cores(array):
    return lax.ppermute(array, "dp", [(i, i ^ 1) for i in range(X * Y * CORES)])


def shift_x(array, k):
    pairs = [
        ((y * X + x) * CORES + c, (y * X + (x + k) % X) * CORES + c)
        for y in range(Y)
        for x in range(X)
        for c in range(CORES)
    ]
    return lax.ppermute(array, "dp", pairs)


def tree_meta(parents, counts, me):
    slot = jnp.arange(SEGMENTS, dtype=jnp.int32)
    mine = slot == me
    row = jnp.concatenate(
        [jnp.where(mine, parents[0, 0], 0), jnp.where(mine, counts[0, 0], 0)]
    )
    near = jnp.maximum(row, jnp.maximum(shift_seq(row, 1), shift_seq(row, 7)))
    full = jnp.maximum(near, jnp.maximum(shift_seq(near, 3), shift_seq(near, 5)))
    return jnp.concatenate([full, jnp.full((SEGMENTS,), me, jnp.int32)])


def attention_grads(queries, keys, values, out_grad, parents, counts):
    me = lax.axis_index("seq")
    q = queries.reshape(SEG_LEN, Q_COLS)
    g = out_grad.reshape(SEG_LEN, Q_COLS)
    own = jnp.concatenate(
        [keys.reshape(SEG_LEN, KV_COLS), values.reshape(SEG_LEN, KV_COLS)], axis=1
    )
    meta = tree_meta(parents, counts, me)
    up, down = own, own
    packets = {0: own}
    for step in range(1, 5):
        down = shift_seq(down, -1)
        packets[step] = down
        if step < 4:
            up = shift_seq(up, 1)
            packets[-step] = up
    stats = add_stats(meta, q, g, [own], [0], None)
    for step in range(1, 4):
        stats = add_stats(
            meta, q, g, [packets[-step], packets[step]], [-step, step], stats
        )
    stats = add_stats(meta, q, g, [packets[4]], [4], stats, last=True)

    def joined(pair):
        return jnp.concatenate([pair[0].astype(F32), pair[1].astype(F32)], axis=1)

    acc, [far] = add_grads(meta, q, g, stats, [packets[4]], [4], None, BF16)
    down = shift_seq(jnp.concatenate(far, axis=1), -1)
    up = None
    for step in range(3, 0, -1):
        acc, [below, above] = add_grads(
            meta, q, g, stats, [packets[-step], packets[step]], [-step, step], acc, F32
        )
        down = shift_seq((joined(below) + down.astype(F32)).astype(BF16), -1)
        if up is None:
            up = joined(above)
        else:
            up = joined(above) + up.astype(F32)
        up = shift_seq(up.astype(BF16), 1)
    dq, [mine] = add_grads(meta, q, g, stats, [own], [0], acc, F32, last=True)
    key_grad = (
        mine[0] + down[:, :KV_COLS].astype(F32) + up[:, :KV_COLS].astype(F32)
    ).astype(BF16)
    value_grad = (
        mine[1] + down[:, KV_COLS:].astype(F32) + up[:, KV_COLS:].astype(F32)
    ).astype(BF16)
    return dq, key_grad, value_grad


def hidden_by_feature(hidden):
    dp = lax.axis_index("dp")
    core = lax.rem(dp, CORES)
    x = lax.rem(lax.div(dp, CORES), X)
    blocks = hidden.reshape(SEG_LEN, Y, X, CORES, HEAD)
    kept = lax.dynamic_index_in_dim(blocks, core, 3, keepdims=False)
    given = lax.dynamic_index_in_dim(blocks, 1 - core, 3, keepdims=False)
    both = jnp.concatenate([kept, swap_cores(given)], axis=0)
    per_x = both.transpose(2, 0, 1, 3).reshape(X, CORES * SEG_LEN, Y * HEAD)
    received = []
    for k in range(X):
        part = lax.dynamic_index_in_dim(per_x, lax.rem(x + k, X), 0, keepdims=False)
        received.append(shift_x(part, k) if k else part)
    return (
        jnp.concatenate([r[:SEG_LEN] for r in received], axis=0),
        jnp.concatenate([r[SEG_LEN:] for r in received], axis=0),
    )


def project_grad(hidden_parts, key_grad):
    tokens = jnp.concatenate(
        [key_grad] + [shift_x(key_grad, k) for k in range(1, X)], axis=0
    )
    others = swap_cores(tokens)
    partial = (dot_tn(hidden_parts[0], tokens) + dot_tn(hidden_parts[1], others)).astype(BF16)
    groups = [
        [((y * X + x) * CORES + c) * SEGMENTS + z for y in range(Y) for z in range(SEGMENTS)]
        for x in range(X)
        for c in range(CORES)
    ]
    rows = lax.all_to_all(
        partial, ("dp", "seq"), 0, 0, axis_index_groups=groups, tiled=True
    )
    return jnp.sum(rows.reshape(Y * SEGMENTS, -1, KV_COLS).astype(F32), axis=0)


def local(hidden_in, queries, keys, values, out_grad, parents, counts):
    hidden_parts = hidden_by_feature(hidden_in.reshape(SEG_LEN, -1))
    dq, key_grad, value_grad = attention_grads(queries, keys, values, out_grad, parents, counts)
    weight_grad = project_grad(hidden_parts, key_grad)
    return (
        dq.reshape(1, 1, SEG_LEN, Q_COLS),
        key_grad.reshape(1, 1, SEG_LEN, KV_COLS),
        value_grad.reshape(1, 1, SEG_LEN, KV_COLS),
        weight_grad,
    )


def solution(mesh):
    wide = P("dp", "seq", None, None)
    return jax.shard_map(
        local,
        mesh=mesh,
        in_specs=(wide, wide, wide, wide, wide, P("dp", "seq"), P("dp", "seq")),
        out_specs=(wide, wide, wide, P(("dp", "seq"), None)),
        check_vma=False,
    )
```

time: 1520 us -> 149 us (0.10)
  the two profiles are of different devices: /device:TPU:0 before, /device:TPU:38 now
where the time goes in v1:
time: 149 us; the launch traced here: 147 us
  starting transfers between devices  49.8 us (33%)
  blocking collectives  32.8 us (22%)
  Pallas kernels  24.8 us (17%)
  waiting for transfers between devices  15.4 us (10%)
  local copies, waits for them, and re-layouts  13.9 us (9%)
  other arithmetic  7.6 us (5%)
  between operations  2.26 us (2%)
    ppermute x18, starting transfers between devices, shift_seq(): lax.ppermute(array, 'seq', [(i, (i + k) % SEGMENTS) for i in range(SEGMEN...  37.8 us
    all_to_all x1, blocking collectives, project_grad(): lax.all_to_all(partial, ('dp', 'seq'), 0, 0, axis_index_groups=groups, ti...  32.8 us
    pallas_call x5, Pallas kernels, add_grads(): pl.pallas_call(functools.partial(grads_kernel, tuple(offsets), first, las...  16.5 us
    ppermute x6, starting transfers between devices, shift_x(): return lax.ppermute(array, 'dp', pairs)  11.9 us
    pallas_call x5, Pallas kernels, add_stats(): pl.pallas_call(functools.partial(stats_kernel, tuple(offsets), first, las...  8.3 us
    ppermute x6, waiting for transfers between devices, shift_x(): return lax.ppermute(array, 'dp', pairs)  8.03 us
    ppermute x18, waiting for transfers between devices, shift_seq(): lax.ppermute(array, 'seq', [(i, (i + k) % SEGMENTS) for i in range(SEGMEN...  7.36 us
    dynamic_slice x2, local copies, waits for them, and re-layouts, hidden_by_feature(): kept = lax.dynamic_index_in_dim(blocks, core, 3, keepdims=False)  4.52 us
  transfers between devices with their start and end apart: 26, of which 10 were waited for; matrix products, arithmetic and copies ran while one was open for 12% of the time, Pallas kernels for 17%

profile of v1, /device:TPU:38, one launch (start us, length us, event | category | flops | bytes accessed | tf_op | source)
XLA Modules:
  0.0 147.4 jit_solution(11970088357753956788)
XLA Ops:
  0.6 1.0 pad_maximum_fusion.1.refs_3_.refs_4_.refs_5_
  1.6 0.2 collective-permute-start.4
  1.8 1.9 %collective-permute-start.8 = (bf16[128,1024]{1,0:T(8,128)(2,1)S(1)}, bf16[128,1024]{1,0:T(8,128)(2,1)S(1)}, u32[]{:S(2)}, u32[]{:S(2)}) collective-permute-start(bf16[128,1024]{1,0:T(8,128)(2,1)S(1)} %pad_maximum_fusion.1.refs_3_.refs_4_.refs_5_), channel_id=1, source_target_pairs={{0,1},{1,2},{2,3},{3,4},{4,5},{5,6},{6,7},{7,0},{8,9},{9,10},{10,1... | collective-permute-start | bytes 786440 | tf_op jit(solution)/shard_map/ppermute | solution.py:273
  5.0 0.1 pad_add_fusion
  5.1 1.9 %collective-permute-start = (s32[16]{0:T(128)S(1)}, s32[16]{0:T(128)S(1)}, u32[]{:S(2)}, u32[]{:S(2)}) collective-permute-start(s32[16]{0:T(128)S(1)} %pad_add_fusion), channel_id=1, source_target_pairs={{0,1},{1,2},{2,3},{3,4},{4,5},{5,6},{6,7},{7,0},{8,9},{9,10},{10,1... | collective-permute-start | bytes 200 | tf_op jit(solution)/shard_map/ppermute | solution.py:273
  7.1 2.1 %collective-permute-start.1 = (s32[16]{0:T(128)S(1)}, s32[16]{0:T(128)S(1)}, u32[]{:S(2)}, u32[]{:S(2)}) collective-permute-start(s32[16]{0:T(128)S(1)} %pad_add_fusion), channel_id=1, source_target_pairs={{0,7},{1,0},{2,1},{3,2},{4,3},{5,4},{6,5},{7,6},{8,15},{9,8},{10,9... | collective-permute-start | bytes 200 | tf_op jit(solution)/shard_map/ppermute | solution.py:273
  9.2 2.3 %copy.15 = bf16[1,1,128,4096]{2,3,1,0:T(8,128)(2,1)} copy(bf16[1,1,128,4096]{3,2,1,0:T(8,128)(2,1)} %param.7) | data formatting | bytes 2097152 | tf_op args[0]
  11.4 3.2 %collective-permute-start.5 = (bf16[128,1024]{1,0:T(8,128)(2,1)S(1)}, bf16[128,1024]{1,0:T(8,128)(2,1)S(1)}, u32[]{:S(2)}, u32[]{:S(2)}) collective-permute-start(bf16[128,1024]{1,0:T(8,128)(2,1)S(1)} %collective-permute-done.4.refs_5_.refs_6_.refs_7_), channel_id=1, source_target_pairs={{0,7},{1,0},{2,1},{3,2},{4,3},{5,4},{6,5},{7,6},{8,15},{9,8},{10,9... | collective-permute-start | bytes 786440 | tf_op jit(solution)/shard_map/ppermute | solution.py:273
  14.7 0.0 copy-start.1
  14.7 2.5 %constant_dynamic-slice_fusion.1 = (bf16[128,4,4,1,128]{0,4,3,2,1:T(8,128)(2,1)}, bf16[128,4,4,1,128]{0,4,3,2,1:T(8,128)(2,1)}) fusion(bf16[128,4,4,2,128]{0,4,3,2,1:T(8,128)(2,1)} %bitcast.52, s32[]{:T(128)S(6)} %select_n.29, s32[]{:T(128)S(6)} %select_n.30), kind=kLoop, calls=%fused_computation.42 | loop fusion | bytes 2097160 | tf_op jit(solution)/shard_map/jit(dynamic_index_in_dim)/dynamic_slice | solution.py:355
  17.2 2.0 %copy.17 = bf16[128,4,4,1,128]{4,0,3,2,1:T(8,128)(2,1)} copy(bf16[128,4,4,1,128]{0,4,3,2,1:T(8,128)(2,1)} %get-tuple-element.52) | data formatting | bytes 1048576 | tf_op jit(solution)/shard_map/jit(dynamic_index_in_dim)/dynamic_slice | solution.py:356
  19.2 2.1 %copy.16 = bf16[128,4,4,1,128]{4,0,3,2,1:T(8,128)(2,1)} copy(bf16[128,4,4,1,128]{0,4,3,2,1:T(8,128)(2,1)} %get-tuple-element.51) | data formatting | bytes 1048576 | tf_op jit(solution)/shard_map/jit(dynamic_index_in_dim)/dynamic_slice | solution.py:355
  21.3 0.1 maximum_maximum_fusion.1
  21.3 3.8 %collective-permute-start.2 = (s32[16]{0:T(128)S(1)}, s32[16]{0:T(128)S(1)}, u32[]{:S(2)}, u32[]{:S(2)}) collective-permute-start(s32[16]{0:T(128)S(1)} %maximum_maximum_fusion.1), channel_id=1, source_target_pairs={{0,3},{1,4},{2,5},{3,6},{4,7},{5,0},{6,1},{7,2},{8,11},{9,12},{10,... | collective-permute-start | bytes 200 | tf_op jit(solution)/shard_map/ppermute | solution.py:273
  25.2 1.2 collective-permute-start.3
  26.4 2.3 %collective-permute-start.6 = (bf16[128,1024]{1,0:T(8,128)(2,1)S(1)}, bf16[128,1024]{1,0:T(8,128)(2,1)S(1)}, u32[]{:S(2)}, u32[]{:S(2)}) collective-permute-start(bf16[128,1024]{1,0:T(8,128)(2,1)S(1)} %collective-permute-done.5.refs_5_.refs_6_.refs_7_), channel_id=1, source_target_pairs={{0,7},{1,0},{2,1},{3,2},{4,3},{5,4},{6,5},{7,6},{8,15},{9,8},{10,9... | collective-permute-start | bytes 786440 | tf_op jit(solution)/shard_map/ppermute | solution.py:273
  28.7 3.0 %collective-permute-done.3 = s32[16]{0:T(128)S(1)} collective-permute-done((s32[16]{0:T(128)S(1)}, s32[16]{0:T(128)S(1)}, u32[]{:S(2)}, u32[]{:S(2)}) %collective-permute-start.3) | collective-permute-done | bytes 96 | tf_op jit(solution)/shard_map/ppermute | solution.py:273
  31.8 2.3 %stats.5.refs_7_ = f32[8,4096]{1,0:T(8,128)S(1)} custom-call(s32[24]{0:T(128)S(1)} %concatenate.44.refs_0_, bf16[128,4096]{1,0:T(8,128)(2,1)S(1)} %bitcast.30, bf16[128,4096]{1,0:T(8,128)(2,1)S(1)} %bitcast.40, bf16[128,1024]{1,0:T(8,128)(2,1)S(1)} %pad_maximum_fusion.1.refs_3_.refs_4_.refs_5_, bf16[128,1024]{1,0:T(8,128)(2,1)S(1)} %pad_maximum_fusion.1.refs_3_.refs_4_.refs_5_), custom_call_target="tpu_custom_call" | custom-call | flops 536870912 | bytes 2097152 | tf_op jit(solution)/shard_map/stats/pallas_call | solution.py:219
  34.1 0.5 collective-permute-done.6.refs_5_.refs_6_.refs_7_
  34.6 2.2 %collective-permute-start.7 = (bf16[128,1024]{1,0:T(8,128)(2,1)S(1)}, bf16[128,1024]{1,0:T(8,128)(2,1)S(1)}, u32[]{:S(2)}, u32[]{:S(2)}) collective-permute-start(bf16[128,1024]{1,0:T(8,128)(2,1)S(1)} %collective-permute-done.6.refs_5_.refs_6_.refs_7_), channel_id=1, source_target_pairs={{0,7},{1,0},{2,1},{3,2},{4,3},{5,4},{6,5},{7,6},{8,15},{9,8},{10,9... | collective-permute-start | bytes 786440 | tf_op jit(solution)/shard_map/ppermute | solution.py:273
  36.8 2.7 %stats.6.refs_7_ = f32[8,4096]{1,0:T(8,128)S(1)} custom-call(s32[24]{0:T(128)S(1)} %concatenate.44.refs_0_, bf16[128,4096]{1,0:T(8,128)(2,1)S(1)} %bitcast.31, bf16[128,4096]{1,0:T(8,128)(2,1)S(1)} %bitcast.41, bf16[128,1024]{1,0:T(8,128)(2,1)S(1)} %collective-permute-done.8.refs_3_.refs_4_.refs_5_, ...), custom_call_target="tpu_custom_call" | custom-call | flops 1073741824 | bytes 2097152 | tf_op jit(solution)/shard_map/stats/pallas_call | solution.py:219
  39.5 1.2 stats.7.refs_7_
  40.7 1.2 stats.8.refs_5_
  41.8 0.4 collective-permute-done.7.refs_3_.refs_4_.refs_5_
  42.2 1.0 stats.9.refs_3_
  43.2 1.3 grads.5
  44.5 2.8 %collective-permute-start.11 = (bf16[128,1024]{1,0:T(8,128)(2,1)S(1)}, bf16[128,1024]{1,0:T(8,128)(2,1)S(1)}, u32[]{:S(2)}, u32[]{:S(2)}) collective-permute-start(bf16[128,1024]{1,0:T(8,128)(2,1)S(1)} %pad_maximum_fusion.2), channel_id=1, source_target_pairs={{0,7},{1,0},{2,1},{3,2},{4,3},{5,4},{6,5},{7,6},{8,15},{9,8},{10,9... | collective-permute-start | bytes 786440 | tf_op jit(solution)/shard_map/ppermute | solution.py:273
  47.3 1.6 %grads.6 = (f32[128,4096]{1,0:T(8,128)S(1)}, f32[128,512]{1,0:T(8,128)S(1)}, f32[128,512]{1,0:T(8,128)S(1)}, f32[128,512]{1,0:T(8,128)S(1)}, f32[128,512]{1,0:T(8,128)S(1)}) custom-call(s32[24]{0:T(128)S(1)} %concatenate.44.refs_0_, bf16[128,4096]{1,0:T(8,128)(2,1)S(1)} %bitcast.36, bf16[128,4096]{1,0:T(8,128)(2,1)S(1)} %bitcast.46, ...), custom_call_target="tpu_custom_call", output_to_operand_aliasing={{0}: (8, {})} | custom-call | flops 2684354560 | bytes 6291456 | tf_op jit(solution)/shard_map/grads/pallas_call | solution.py:253
  49.0 0.1 collective-permute-start.15
  49.1 2.2 %collective-permute-done.11 = bf16[128,1024]{1,0:T(8,128)(2,1)S(1)} collective-permute-done((bf16[128,1024]{1,0:T(8,128)(2,1)S(1)}, bf16[128,1024]{1,0:T(8,128)(2,1)S(1)}, u32[]{:S(2)}, u32[]{:S(2)}) %collective-permute-start.11) | collective-permute-done | bytes 262176 | tf_op jit(solution)/shard_map/ppermute | solution.py:273
  51.3 0.1 fusion.3
  51.4 4.7 %collective-permute-start.12 = (bf16[128,1024]{1,0:T(8,128)(2,1)S(1)}, bf16[128,1024]{1,0:T(8,128)(2,1)S(1)}, u32[]{:S(2)}, u32[]{:S(2)}) collective-permute-start(bf16[128,1024]{1,0:T(8,128)(2,1)S(1)} %fusion.3), channel_id=1, source_target_pairs={{0,7},{1,0},{2,1},{3,2},{4,3},{5,4},{6,5},{7,6},{8,15},{9,8},{10,9... | collective-permute-start | bytes 786440 | tf_op jit(solution)/shard_map/ppermute | solution.py:273
  56.1 1.6 %grads.7 = (f32[128,4096]{1,0:T(8,128)S(1)}, f32[128,512]{1,0:T(8,128)S(1)}, f32[128,512]{1,0:T(8,128)S(1)}, f32[128,512]{1,0:T(8,128)S(1)}, f32[128,512]{1,0:T(8,128)S(1)}) custom-call(s32[24]{0:T(128)S(1)} %concatenate.44.refs_0_, bf16[128,4096]{1,0:T(8,128)(2,1)S(1)} %bitcast.37, bf16[128,4096]{1,0:T(8,128)(2,1)S(1)} %bitcast.47, ...), custom_call_target="tpu_custom_call", output_to_operand_aliasing={{0}: (8, {})} | custom-call | flops 2684354560 | bytes 6291456 | tf_op jit(solution)/shard_map/grads/pallas_call | solution.py:253
  57.7 0.5 collective-permute-done.15
  58.2 0.1 fusion.5
  58.3 3.2 %collective-permute-start.16 = (bf16[128,1024]{1,0:T(8,128)(2,1)S(1)}, bf16[128,1024]{1,0:T(8,128)(2,1)S(1)}, u32[]{:S(2)}, u32[]{:S(2)}) collective-permute-start(bf16[128,1024]{1,0:T(8,128)(2,1)S(1)} %fusion.5), channel_id=1, source_target_pairs={{0,1},{1,2},{2,3},{3,4},{4,5},{5,6},{6,7},{7,0},{8,9},{9,10},{10,1... | collective-permute-start | bytes 786440 | tf_op jit(solution)/shard_map/ppermute | solution.py:273
  61.5 0.1 fusion.2
  61.6 2.4 %collective-permute-start.13 = (bf16[128,1024]{1,0:T(8,128)(2,1)S(1)}, bf16[128,1024]{1,0:T(8,128)(2,1)S(1)}, u32[]{:S(2)}, u32[]{:S(2)}) collective-permute-start(bf16[128,1024]{1,0:T(8,128)(2,1)S(1)} %fusion.2), channel_id=1, source_target_pairs={{0,7},{1,0},{2,1},{3,2},{4,3},{5,4},{6,5},{7,6},{8,15},{9,8},{10,9... | collective-permute-start | bytes 786440 | tf_op jit(solution)/shard_map/ppermute | solution.py:273
  64.0 6.0 %grads.8 = (f32[128,4096]{1,0:T(8,128)S(1)}, f32[128,512]{1,0:T(8,128)S(1)}, f32[128,512]{1,0:T(8,128)S(1)}, f32[128,512]{1,0:T(8,128)S(1)}, f32[128,512]{1,0:T(8,128)S(1)}) custom-call(s32[24]{0:T(128)S(1)} %concatenate.44.refs_0_, bf16[128,4096]{1,0:T(8,128)(2,1)S(1)} %bitcast.38, bf16[128,4096]{1,0:T(8,128)(2,1)S(1)} %bitcast.48, ...), custom_call_target="tpu_custom_call", output_to_operand_aliasing={{0}: (8, {})} | custom-call | flops 2684354560 | bytes 6291456 | tf_op jit(solution)/shard_map/grads/pallas_call | solution.py:253
  70.0 0.7 fusion.4
  70.7 0.1 collective-permute-start.17
  70.9 0.7 collective-permute-done.13
  71.6 0.8 fusion.1
  72.4 5.5 %collective-permute-start.14 = (bf16[128,1024]{1,0:T(8,128)(2,1)}, bf16[128,1024]{1,0:T(8,128)(2,1)}, u32[]{:S(2)}, u32[]{:S(2)}) collective-permute-start(bf16[128,1024]{1,0:T(8,128)(2,1)} %fusion.1), channel_id=1, source_target_pairs={{0,7},{1,0},{2,1},{3,2},{4,3},{5,4},{6,5},{7,6},{8,15},{9,8},{10,9... | collective-permute-start | bytes 786440 | tf_op jit(solution)/shard_map/ppermute | solution.py:273
  77.9 2.1 %maximum_bitcast_fusion = bf16[4,256,4,128]{3,1,0,2:T(8,128)(2,1)} fusion(bf16[128,4,4,128]{3,0,2,1:T(8,128)(2,1)} %collective-permute-done.18, bf16[128,4,4,128]{3,0,2,1:T(8,128)(2,1)S(1)} %bitcast.53), kind=kLoop, calls=%fused_computation.2 | loop fusion | flops 2097152 | bytes 2097152 | tf_op jit(solution)/shard_map/transpose | solution.py:358
  80.0 1.5 %copy.18 = bf16[4,256,4,128]{1,3,2,0:T(8,128)(2,1)S(1)} copy(bf16[4,256,4,128]{3,1,0,2:T(8,128)(2,1)} %maximum_bitcast_fusion) | data formatting | bytes 2097152 | tf_op jit(solution)/shard_map/transpose | solution.py:358
  81.5 0.9 dynamic-slice_bitcast_fusion.2
  82.4 5.7 %collective-permute-start.19 = (bf16[256,512]{0,1:T(8,128)(2,1)}, bf16[256,512]{0,1:T(8,128)(2,1)}, u32[]{:S(2)}, u32[]{:S(2)}) collective-permute-start(bf16[256,512]{0,1:T(8,128)(2,1)} %get-tuple-element.48), channel_id=1, source_target_pairs={{0,16},{8,24},{16,32},{24,40},{32,48},{40,56},{48,0},{56,8},{64,80... | collective-permute-start | bytes 786440 | tf_op jit(solution)/shard_map/ppermute | solution.py:287
  88.1 1.6 %copy-done.3 = f32[128,4096]{1,0:T(8,128)S(1)} copy-done((f32[128,4096]{1,0:T(8,128)S(1)}, f32[128,4096]{1,0:T(8,128)}, u32[]{:S(2)}) %copy-start.3) | copy-done | bytes 2097176
  89.7 6.0 %grads.9 = (bf16[128,4096]{1,0:T(8,128)(2,1)}, f32[128,512]{1,0:T(8,128)S(1)}, f32[128,512]{1,0:T(8,128)S(1)}) custom-call(s32[24]{0:T(128)S(1)} %concatenate.44.refs_0_, bf16[128,4096]{1,0:T(8,128)(2,1)S(1)} %bitcast.39, bf16[128,4096]{1,0:T(8,128)(2,1)S(1)} %bitcast.49, f32[8,4096]{1,0:T(8,128)S(1)} %stats.9.refs_3_, ...), custom_call_target="tpu_custom_call" | custom-call | flops 1342177280 | bytes 6291456 | tf_op jit(solution)/shard_map/grads/pallas_call | solution.py:253
  95.7 1.9 %fusion.21 = (bf16[1,1,128,512]{3,2,1,0:T(8,128)(2,1)}, bf16[128,512]{1,0:T(8,128)(2,1)S(1)}) fusion(f32[128,512]{1,0:T(8,128)S(1)} %get-tuple-element.45, bf16[128,1024]{1,0:T(8,128)(2,1)} %collective-permute-done.17, bf16[128,1024]{1,0:T(8,128)(2,1)} %collective-permute-done.14, f32[128,512]{1,0:T(8,128)S(1)} %get-tuple-element.30), kind=kLoop, calls=%fused_computation.38 | loop fusion | flops 655360 | bytes 1310720 | tf_op jit(solution)/shard_map/reshape | solution.py:393
  97.6 2.0 %collective-permute-start.24 = (bf16[128,512]{1,0:T(8,128)(2,1)S(1)}, bf16[128,512]{1,0:T(8,128)(2,1)S(1)}, u32[]{:S(2)}, u32[]{:S(2)}) collective-permute-start(bf16[128,512]{1,0:T(8,128)(2,1)S(1)} %get-tuple-element.54), channel_id=1, source_target_pairs={{0,48},{8,56},{16,0},{24,8},{32,16},{40,24},{48,32},{56,40},{64,11... | collective-permute-start | bytes 393224 | tf_op jit(solution)/shard_map/ppermute | solution.py:287
  99.6 4.1 %collective-permute-start.20 = (bf16[256,512]{0,1:T(8,128)(2,1)}, bf16[256,512]{0,1:T(8,128)(2,1)S(1)}, u32[]{:S(2)}, u32[]{:S(2)}) collective-permute-start(bf16[256,512]{0,1:T(8,128)(2,1)} %get-tuple-element.50), channel_id=1, source_target_pairs={{0,32},{8,40},{16,48},{24,56},{32,0},{40,8},{48,16},{56,24},{64,96... | collective-permute-start | bytes 786440 | tf_op jit(solution)/shard_map/ppermute | solution.py:287
  103.8 0.1 collective-permute-start.21
  103.8 1.7 %collective-permute-done.23 = bf16[128,512]{1,0:T(8,128)(2,1)S(1)} collective-permute-done((bf16[128,512]{1,0:T(8,128)(2,1)S(1)}, bf16[128,512]{1,0:T(8,128)(2,1)S(1)}, u32[]{:S(2)}, u32[]{:S(2)}) %collective-permute-start.23) | collective-permute-done | bytes 131104 | tf_op jit(solution)/shard_map/ppermute | solution.py:287
  105.5 1.9 %collective-permute-done.24 = bf16[128,512]{1,0:T(8,128)(2,1)S(1)} collective-permute-done((bf16[128,512]{1,0:T(8,128)(2,1)S(1)}, bf16[128,512]{1,0:T(8,128)(2,1)S(1)}, u32[]{:S(2)}, u32[]{:S(2)}) %collective-permute-start.24) | collective-permute-done | bytes 131104 | tf_op jit(solution)/shard_map/ppermute | solution.py:287
  107.4 0.1 collective-permute-start.25
  107.5 1.0 fusion.24
  108.5 1.8 %collective-permute-done.20 = bf16[256,512]{0,1:T(8,128)(2,1)S(1)} collective-permute-done((bf16[256,512]{0,1:T(8,128)(2,1)}, bf16[256,512]{0,1:T(8,128)(2,1)S(1)}, u32[]{:S(2)}, u32[]{:S(2)}) %collective-permute-start.20) | collective-permute-done | bytes 262176 | tf_op jit(solution)/shard_map/ppermute | solution.py:287
  110.4 2.7 %collective-permute-done.21 = bf16[256,512]{0,1:T(8,128)(2,1)S(1)} collective-permute-done((bf16[256,512]{0,1:T(8,128)(2,1)}, bf16[256,512]{0,1:T(8,128)(2,1)S(1)}, u32[]{:S(2)}, u32[]{:S(2)}) %collective-permute-start.21) | collective-permute-done | bytes 262176 | tf_op jit(solution)/shard_map/ppermute | solution.py:287
  113.1 0.4 fusion.13
  113.5 0.4 fusion
  114.0 32.8 %all_to_all.9 = bf16[32,16,512]{2,1,0:T(8,128)(2,1)S(1)} all-to-all(bf16[32,16,512]{2,1,0:T(8,128)(2,1)S(1)} %bitcast.55), channel_id=1, replica_groups={{0,1,2,3,4,5,6,7,64,65,66,67,68,69,70,71,128,129,130,131,132,133,134,13..., dimensions={0} | all-to-all | bytes 1048576 | tf_op jit(solution)/shard_map/all_to_all | solution.py:380
  146.7 0.7 convert_reduce_fusion
  (42 shorter events, 0.3 us)
Async XLA Ops:
  1.6 9.8 %collective-permute-start.4 = (bf16[128,1024]{1,0:T(8,128)(2,1)S(1)}, bf16[128,1024]{1,0:T(8,128)(2,1)S(1)}, u32[]{:S(2)}, u32[]{:S(2)}) collective-permute-start(bf16[128,1024]{1,0:T(8,128)(2,1)S(1)} %pad_maximum_fusion.1.refs_3_.refs_4_.refs_5_), channel_id=1, source_target_pairs={{0,7},{1,0},{2,1},{3,2},{4,3},{5,4},{6,5},{7,6},{8,15},{9,8},{10,9... | collective-permute-start | bytes 786440 | tf_op jit(solution)/shard_map/ppermute | solution.py:273
  1.8 12.8 %collective-permute-start.8 = (bf16[128,1024]{1,0:T(8,128)(2,1)S(1)}, bf16[128,1024]{1,0:T(8,128)(2,1)S(1)}, u32[]{:S(2)}, u32[]{:S(2)}) collective-permute-start(bf16[128,1024]{1,0:T(8,128)(2,1)S(1)} %pad_maximum_fusion.1.refs_3_.refs_4_.refs_5_), channel_id=1, source_target_pairs={{0,1},{1,2},{2,3},{3,4},{4,5},{5,6},{6,7},{7,0},{8,9},{9,10},{10,1... | collective-permute-start | bytes 786440 | tf_op jit(solution)/shard_map/ppermute | solution.py:273
  5.1 16.1 %collective-permute-start = (s32[16]{0:T(128)S(1)}, s32[16]{0:T(128)S(1)}, u32[]{:S(2)}, u32[]{:S(2)}) collective-permute-start(s32[16]{0:T(128)S(1)} %pad_add_fusion), channel_id=1, source_target_pairs={{0,1},{1,2},{2,3},{3,4},{4,5},{5,6},{6,7},{7,0},{8,9},{9,10},{10,1... | collective-permute-start | bytes 200 | tf_op jit(solution)/shard_map/ppermute | solution.py:273
  7.1 14.2 %collective-permute-start.1 = (s32[16]{0:T(128)S(1)}, s32[16]{0:T(128)S(1)}, u32[]{:S(2)}, u32[]{:S(2)}) collective-permute-start(s32[16]{0:T(128)S(1)} %pad_add_fusion), channel_id=1, source_target_pairs={{0,7},{1,0},{2,1},{3,2},{4,3},{5,4},{6,5},{7,6},{8,15},{9,8},{10,9... | collective-permute-start | bytes 200 | tf_op jit(solution)/shard_map/ppermute | solution.py:273
  11.4 15.0 %collective-permute-start.5 = (bf16[128,1024]{1,0:T(8,128)(2,1)S(1)}, bf16[128,1024]{1,0:T(8,128)(2,1)S(1)}, u32[]{:S(2)}, u32[]{:S(2)}) collective-permute-start(bf16[128,1024]{1,0:T(8,128)(2,1)S(1)} %collective-permute-done.4.refs_5_.refs_6_.refs_7_), channel_id=1, source_target_pairs={{0,7},{1,0},{2,1},{3,2},{4,3},{5,4},{6,5},{7,6},{8,15},{9,8},{10,9... | collective-permute-start | bytes 786440 | tf_op jit(solution)/shard_map/ppermute | solution.py:273
  14.7 14.0 %collective-permute-start.9 = (bf16[128,1024]{1,0:T(8,128)(2,1)S(1)}, bf16[128,1024]{1,0:T(8,128)(2,1)S(1)}, u32[]{:S(2)}, u32[]{:S(2)}) collective-permute-start(bf16[128,1024]{1,0:T(8,128)(2,1)S(1)} %collective-permute-done.8.refs_3_.refs_4_.refs_5_), channel_id=1, source_target_pairs={{0,1},{1,2},{2,3},{3,4},{4,5},{5,6},{6,7},{7,0},{8,9},{9,10},{10,1... | collective-permute-start | bytes 786440 | tf_op jit(solution)/shard_map/ppermute | solution.py:273
  14.7 17.1 %copy-start = (bf16[1,1,128,4096]{3,2,1,0:T(8,128)(2,1)S(1)}, bf16[1,1,128,4096]{3,2,1,0:T(8,128)(2,1)}, u32[]{:S(2)}) copy-start(bf16[1,1,128,4096]{3,2,1,0:T(8,128)(2,1)} %param.8) | copy-start | bytes 3145732
  14.7 17.1 %copy-start.1 = (bf16[1,1,128,4096]{3,2,1,0:T(8,128)(2,1)S(1)}, bf16[1,1,128,4096]{3,2,1,0:T(8,128)(2,1)}, u32[]{:S(2)}) copy-start(bf16[1,1,128,4096]{3,2,1,0:T(8,128)(2,1)} %param.11) | copy-start | bytes 3145732
  19.2 58.7 %collective-permute-start.18 = (bf16[128,4,4,128]{3,0,2,1:T(8,128)(2,1)}, bf16[128,4,4,128]{3,0,2,1:T(8,128)(2,1)}, u32[]{:S(2)}, u32[]{:S(2)}) collective-permute-start(bf16[128,4,4,128]{3,0,2,1:T(8,128)(2,1)} %bitcast.54), channel_id=1, source_target_pairs={{0,8},{8,0},{16,24},{24,16},{32,40},{40,32},{48,56},{56,48},{64,72... | collective-permute-start | bytes 1572872 | tf_op jit(solution)/shard_map/ppermute | solution.py:277
  21.3 7.3 %collective-permute-start.2 = (s32[16]{0:T(128)S(1)}, s32[16]{0:T(128)S(1)}, u32[]{:S(2)}, u32[]{:S(2)}) collective-permute-start(s32[16]{0:T(128)S(1)} %maximum_maximum_fusion.1), channel_id=1, source_target_pairs={{0,3},{1,4},{2,5},{3,6},{4,7},{5,0},{6,1},{7,2},{8,11},{9,12},{10,... | collective-permute-start | bytes 200 | tf_op jit(solution)/shard_map/ppermute | solution.py:273
  25.2 6.6 %collective-permute-start.3 = (s32[16]{0:T(128)S(1)}, s32[16]{0:T(128)S(1)}, u32[]{:S(2)}, u32[]{:S(2)}) collective-permute-start(s32[16]{0:T(128)S(1)} %maximum_maximum_fusion.1), channel_id=1, source_target_pairs={{0,5},{1,6},{2,7},{3,0},{4,1},{5,2},{6,3},{7,4},{8,13},{9,14},{10,... | collective-permute-start | bytes 200 | tf_op jit(solution)/shard_map/ppermute | solution.py:273
  26.4 8.2 %collective-permute-start.6 = (bf16[128,1024]{1,0:T(8,128)(2,1)S(1)}, bf16[128,1024]{1,0:T(8,128)(2,1)S(1)}, u32[]{:S(2)}, u32[]{:S(2)}) collective-permute-start(bf16[128,1024]{1,0:T(8,128)(2,1)S(1)} %collective-permute-done.5.refs_5_.refs_6_.refs_7_), channel_id=1, source_target_pairs={{0,7},{1,0},{2,1},{3,2},{4,3},{5,4},{6,5},{7,6},{8,15},{9,8},{10,9... | collective-permute-start | bytes 786440 | tf_op jit(solution)/shard_map/ppermute | solution.py:273
  28.7 12.0 %collective-permute-start.10 = (bf16[128,1024]{1,0:T(8,128)(2,1)S(1)}, bf16[128,1024]{1,0:T(8,128)(2,1)S(1)}, u32[]{:S(2)}, u32[]{:S(2)}) collective-permute-start(bf16[128,1024]{1,0:T(8,128)(2,1)S(1)} %collective-permute-done.9.refs_3_.refs_4_.refs_5_), channel_id=1, source_target_pairs={{0,1},{1,2},{2,3},{3,4},{4,5},{5,6},{6,7},{7,0},{8,9},{9,10},{10,1... | collective-permute-start | bytes 786440 | tf_op jit(solution)/shard_map/ppermute | solution.py:273
  34.6 7.6 %collective-permute-start.7 = (bf16[128,1024]{1,0:T(8,128)(2,1)S(1)}, bf16[128,1024]{1,0:T(8,128)(2,1)S(1)}, u32[]{:S(2)}, u32[]{:S(2)}) collective-permute-start(bf16[128,1024]{1,0:T(8,128)(2,1)S(1)} %collective-permute-done.6.refs_5_.refs_6_.refs_7_), channel_id=1, source_target_pairs={{0,7},{1,0},{2,1},{3,2},{4,3},{5,4},{6,5},{7,6},{8,15},{9,8},{10,9... | collective-permute-start | bytes 786440 | tf_op jit(solution)/shard_map/ppermute | solution.py:273
  44.5 6.8 %collective-permute-start.11 = (bf16[128,1024]{1,0:T(8,128)(2,1)S(1)}, bf16[128,1024]{1,0:T(8,128)(2,1)S(1)}, u32[]{:S(2)}, u32[]{:S(2)}) collective-permute-start(bf16[128,1024]{1,0:T(8,128)(2,1)S(1)} %pad_maximum_fusion.2), channel_id=1, source_target_pairs={{0,7},{1,0},{2,1},{3,2},{4,3},{5,4},{6,5},{7,6},{8,15},{9,8},{10,9... | collective-permute-start | bytes 786440 | tf_op jit(solution)/shard_map/ppermute | solution.py:273
  49.0 9.2 %collective-permute-start.15 = (bf16[128,1024]{1,0:T(8,128)(2,1)S(1)}, bf16[128,1024]{1,0:T(8,128)(2,1)S(1)}, u32[]{:S(2)}, u32[]{:S(2)}) collective-permute-start(bf16[128,1024]{1,0:T(8,128)(2,1)S(1)} %pad_maximum_fusion.3), channel_id=1, source_target_pairs={{0,1},{1,2},{2,3},{3,4},{4,5},{5,6},{6,7},{7,0},{8,9},{9,10},{10,1... | collective-permute-start | bytes 786440 | tf_op jit(solution)/shard_map/ppermute | solution.py:273
  51.4 10.2 %collective-permute-start.12 = (bf16[128,1024]{1,0:T(8,128)(2,1)S(1)}, bf16[128,1024]{1,0:T(8,128)(2,1)S(1)}, u32[]{:S(2)}, u32[]{:S(2)}) collective-permute-start(bf16[128,1024]{1,0:T(8,128)(2,1)S(1)} %fusion.3), channel_id=1, source_target_pairs={{0,7},{1,0},{2,1},{3,2},{4,3},{5,4},{6,5},{7,6},{8,15},{9,8},{10,9... | collective-permute-start | bytes 786440 | tf_op jit(solution)/shard_map/ppermute | solution.py:273
  58.3 11.7 %collective-permute-start.16 = (bf16[128,1024]{1,0:T(8,128)(2,1)S(1)}, bf16[128,1024]{1,0:T(8,128)(2,1)S(1)}, u32[]{:S(2)}, u32[]{:S(2)}) collective-permute-start(bf16[128,1024]{1,0:T(8,128)(2,1)S(1)} %fusion.5), channel_id=1, source_target_pairs={{0,1},{1,2},{2,3},{3,4},{4,5},{5,6},{6,7},{7,0},{8,9},{9,10},{10,1... | collective-permute-start | bytes 786440 | tf_op jit(solution)/shard_map/ppermute | solution.py:273
  61.6 10.0 %collective-permute-start.13 = (bf16[128,1024]{1,0:T(8,128)(2,1)S(1)}, bf16[128,1024]{1,0:T(8,128)(2,1)S(1)}, u32[]{:S(2)}, u32[]{:S(2)}) collective-permute-start(bf16[128,1024]{1,0:T(8,128)(2,1)S(1)} %fusion.2), channel_id=1, source_target_pairs={{0,7},{1,0},{2,1},{3,2},{4,3},{5,4},{6,5},{7,6},{8,15},{9,8},{10,9... | collective-permute-start | bytes 786440 | tf_op jit(solution)/shard_map/ppermute | solution.py:273
  70.0 2.4 %copy-start.2 = (f32[128,4096]{1,0:T(8,128)}, f32[128,4096]{1,0:T(8,128)S(1)}, u32[]{:S(2)}) copy-start(f32[128,4096]{1,0:T(8,128)S(1)} %get-tuple-element.28.refs_6_) | copy-start | bytes 6291460
  70.0 7.9 %copy-start.4 = (bf16[128,4,4,1,128]{4,0,3,2,1:T(8,128)(2,1)S(1)}, bf16[128,4,4,1,128]{4,0,3,2,1:T(8,128)(2,1)}, u32[]{:S(2)}) copy-start(bf16[128,4,4,1,128]{4,0,3,2,1:T(8,128)(2,1)} %copy.16) | copy-start | bytes 1572868
  70.7 24.9 %collective-permute-start.17 = (bf16[128,1024]{1,0:T(8,128)(2,1)}, bf16[128,1024]{1,0:T(8,128)(2,1)}, u32[]{:S(2)}, u32[]{:S(2)}) collective-permute-start(bf16[128,1024]{1,0:T(8,128)(2,1)} %fusion.4), channel_id=1, source_target_pairs={{0,1},{1,2},{2,3},{3,4},{4,5},{5,6},{6,7},{7,0},{8,9},{9,10},{10,1... | collective-permute-start | bytes 786440 | tf_op jit(solution)/shard_map/ppermute | solution.py:273
  72.4 23.3 %collective-permute-start.14 = (bf16[128,1024]{1,0:T(8,128)(2,1)}, bf16[128,1024]{1,0:T(8,128)(2,1)}, u32[]{:S(2)}, u32[]{:S(2)}) collective-permute-start(bf16[128,1024]{1,0:T(8,128)(2,1)} %fusion.1), channel_id=1, source_target_pairs={{0,7},{1,0},{2,1},{3,2},{4,3},{5,4},{6,5},{7,6},{8,15},{9,8},{10,9... | collective-permute-start | bytes 786440 | tf_op jit(solution)/shard_map/ppermute | solution.py:273
  82.4 25.1 %collective-permute-start.19 = (bf16[256,512]{0,1:T(8,128)(2,1)}, bf16[256,512]{0,1:T(8,128)(2,1)}, u32[]{:S(2)}, u32[]{:S(2)}) collective-permute-start(bf16[256,512]{0,1:T(8,128)(2,1)} %get-tuple-element.48), channel_id=1, source_target_pairs={{0,16},{8,24},{16,32},{24,40},{32,48},{40,56},{48,0},{56,8},{64,80... | collective-permute-start | bytes 786440 | tf_op jit(solution)/shard_map/ppermute | solution.py:287
  88.1 1.6 %copy-start.3 = (f32[128,4096]{1,0:T(8,128)S(1)}, f32[128,4096]{1,0:T(8,128)}, u32[]{:S(2)}) copy-start(f32[128,4096]{1,0:T(8,128)} %copy-done.2) | copy-start | bytes 6291460
  97.6 16.0 %copy-start.5 = (bf16[128,512]{1,0:T(8,128)(2,1)}, bf16[128,512]{1,0:T(8,128)(2,1)S(1)}, u32[]{:S(2)}) copy-start(bf16[128,512]{1,0:T(8,128)(2,1)S(1)} %get-tuple-element.54) | copy-start | bytes 393220
  97.6 6.2 %collective-permute-start.22 = (bf16[128,512]{1,0:T(8,128)(2,1)S(1)}, bf16[128,512]{1,0:T(8,128)(2,1)S(1)}, u32[]{:S(2)}, u32[]{:S(2)}) collective-permute-start(bf16[128,512]{1,0:T(8,128)(2,1)S(1)} %get-tuple-element.54), channel_id=1, source_target_pairs={{0,16},{8,24},{16,32},{24,40},{32,48},{40,56},{48,0},{56,8},{64,80... | collective-permute-start | bytes 393224 | tf_op jit(solution)/shard_map/ppermute | solution.py:287
  97.6 7.9 %collective-permute-start.23 = (bf16[128,512]{1,0:T(8,128)(2,1)S(1)}, bf16[128,512]{1,0:T(8,128)(2,1)S(1)}, u32[]{:S(2)}, u32[]{:S(2)}) collective-permute-start(bf16[128,512]{1,0:T(8,128)(2,1)S(1)} %get-tuple-element.54), channel_id=1, source_target_pairs={{0,32},{8,40},{16,48},{24,56},{32,0},{40,8},{48,16},{56,24},{64,96... | collective-permute-start | bytes 393224 | tf_op jit(solution)/shard_map/ppermute | solution.py:287
  97.6 9.8 %collective-permute-start.24 = (bf16[128,512]{1,0:T(8,128)(2,1)S(1)}, bf16[128,512]{1,0:T(8,128)(2,1)S(1)}, u32[]{:S(2)}, u32[]{:S(2)}) collective-permute-start(bf16[128,512]{1,0:T(8,128)(2,1)S(1)} %get-tuple-element.54), channel_id=1, source_target_pairs={{0,48},{8,56},{16,0},{24,8},{32,16},{40,24},{48,32},{56,40},{64,11... | collective-permute-start | bytes 393224 | tf_op jit(solution)/shard_map/ppermute | solution.py:287
  99.6 10.7 %collective-permute-start.20 = (bf16[256,512]{0,1:T(8,128)(2,1)}, bf16[256,512]{0,1:T(8,128)(2,1)S(1)}, u32[]{:S(2)}, u32[]{:S(2)}) collective-permute-start(bf16[256,512]{0,1:T(8,128)(2,1)} %get-tuple-element.50), channel_id=1, source_target_pairs={{0,32},{8,40},{16,48},{24,56},{32,0},{40,8},{48,16},{56,24},{64,96... | collective-permute-start | bytes 786440 | tf_op jit(solution)/shard_map/ppermute | solution.py:287
  103.8 9.3 %collective-permute-start.21 = (bf16[256,512]{0,1:T(8,128)(2,1)}, bf16[256,512]{0,1:T(8,128)(2,1)S(1)}, u32[]{:S(2)}, u32[]{:S(2)}) collective-permute-start(bf16[256,512]{0,1:T(8,128)(2,1)} %get-tuple-element.49), channel_id=1, source_target_pairs={{0,48},{8,56},{16,0},{24,8},{32,16},{40,24},{48,32},{56,40},{64,11... | collective-permute-start | bytes 786440 | tf_op jit(solution)/shard_map/ppermute | solution.py:287
  107.4 5.6 %collective-permute-start.25 = (bf16[512,512]{1,0:T(8,128)(2,1)S(1)}, bf16[512,512]{1,0:T(8,128)(2,1)S(1)}, u32[]{:S(2)}, u32[]{:S(2)}) collective-permute-start(bf16[512,512]{1,0:T(8,128)(2,1)S(1)} %pad_maximum_fusion), channel_id=1, source_target_pairs={{0,8},{8,0},{16,24},{24,16},{32,40},{40,32},{48,56},{56,48},{64,72... | collective-permute-start | bytes 1572872 | tf_op jit(solution)/shard_map/ppermute | solution.py:277
